TPU v7x, 32 devices: a whole 2x2x4 slice. The times are simulated.
32 devices in a mesh: inner: 4 (over x, core), outer: 8 (over z, y).
Axes of the slice: x: 2, y: 2, z: 4, core: 2. Of those that a mesh axis runs over, the one named last changes fastest.
Arguments:
- out_grad: bfloat16 [4096, 2048], P(('inner', 'outer')), may hold values from -6 to 6
- expert_ids: int32 [4096, 8], P(('inner', 'outer')), may hold values from 0 to 31, all different within a row; in each aligned block of 128 rows (0 to 127, 128 to 255, ...) at most 40 rows name the same one
- gates: float32 [4096, 8], P(('inner', 'outer')), may hold values from 0.05 to 0.5
- expert_input: bfloat16 [32, 32, 40, 2048], P(None, ('inner', 'outer')), may hold values from -6 to 6
- gate_up_weight: bfloat16 [32, 2048, 1536], P(('inner', 'outer')), may hold values from -0.125 to 0.125
- down_weight: bfloat16 [32, 768, 2048], P(('inner', 'outer')), may hold values from -0.21875 to 0.21875
Outputs:
- token_grad: bfloat16 [4096, 2048], P(('inner', 'outer'))
- down_grad: bfloat16 [32, 768, 2048], P(('inner', 'outer'))
Inputs may be any that keep to these rules, and one draw needn't show every extreme that they name: `expert_ids`: within each aligned block of 128 tokens (the tokens of one device) the 8 experts of a token differ, no expert is named by more than 40 pairs, a bound that some block reaches; every expert is named somewhere.
All inputs are finite; a program needn't handle non-finite values.
Results may differ from a plain program's by a relative error of at most 0.0064.
Values may be sent and summed in bfloat16 or wider, within the bound.
A program may use at most 128 MiB of HBM per device.

v0:
```python
import functools

import jax
import jax.numpy as jnp
from jax import lax
from jax.experimental import pallas as pl
from jax.experimental.pallas import tpu as pltpu
from jax.sharding import Mesh, PartitionSpec as P

PLANE = ("i", "n")
MESH = pl.DeviceIdType.MESH
F32, BF16 = jnp.float32, jnp.bfloat16
LANES = 512


def fused_kernel(
    cps, og_in, maps_in, x_in, wgu_in, wd_in, token_out, down_out,
    og, maps, pick, scale, send, rows, xs, back, pre, wgu, wd, dgu, hid, own, part, got,
    load_sem, copy_sem, zs_sem, zr_sem, ms_sem, mr_sem, ds_sem, dr_sem, cs_sem, cr_sem, ps_sem, pr_sem,
):
    i, m, n = lax.axis_index("i"), lax.axis_index("m"), lax.axis_index("n")
    x, c = i // 2, i % 2
    zh, zl = m // 2, m % 2
    mine = i * 2 + n
    tok, width = og_in.shape
    hidden_width = wd_in.shape[0]
    pair = 2 * cps
    total = 8 * pair
    early = cps // 16 * 16
    late = pair - early
    early_at = pl.multiple_of(zl * late, 16)
    late_at = pl.multiple_of((1 - zl) * early, 16)

    def z_peer(j):
        return 2 * ((zh + j // 2) % 2) + (zl + j % 2) % 2

    def plane_peer(k):
        ki, kc, kn = k // 4, k // 2 % 2, k % 2
        return 2 * ((x + ki) % 2) + (c + kc) % 2, (n + kn) % 2

    def block_rows(which):
        return pl.ds(pl.multiple_of(which * tok, tok), tok)

    loads = [
        pltpu.make_async_copy(og_in, og.at[0, block_rows(zl)], load_sem.at[0]),
        pltpu.make_async_copy(maps_in.at[m], maps.at[0, zl], load_sem.at[1]),
        pltpu.make_async_copy(wgu_in, wgu, load_sem.at[2]),
    ]
    for g in range(2):
        for a in range(4):
            loads.append(
                pltpu.make_async_copy(
                    x_in.at[a, pl.ds(2 * ((zh + g) % 2), 2)],
                    xs.at[g, pl.ds(2 * a, 2)],
                    load_sem.at[3 + 4 * g + a],
                )
            )
    loads.append(pltpu.make_async_copy(wd_in, wd, load_sem.at[11]))
    for load in loads:
        load.start()

    barrier = pltpu.get_barrier_semaphore()
    for j in range(1, 4):
        pl.semaphore_signal(barrier, inc=1, device_id=(i, z_peer(j), n), device_id_type=MESH)
    for k in range(1, 8):
        pi, pn = plane_peer(k)
        pl.semaphore_signal(barrier, inc=1, device_id=(pi, m, pn), device_id_type=MESH)
    pl.semaphore_wait(barrier, 10)

    map_copies, block_copies = [], []
    for j in range(1, 4):
        there = z_peer(j)
        map_copies.append(
            pltpu.make_async_remote_copy(
                src_ref=maps_in.at[there], dst_ref=maps.at[j // 2, zl],
                send_sem=ms_sem.at[j], recv_sem=mr_sem.at[j],
                device_id=(i, there, n), device_id_type=MESH,
            )
        )
        block_copies.append(
            pltpu.make_async_remote_copy(
                src_ref=og_in, dst_ref=og.at[j // 2, block_rows(zl)],
                send_sem=zs_sem.at[j], recv_sem=zr_sem.at[j],
                device_id=(i, there, n), device_id_type=MESH,
            )
        )
    for copy in map_copies + block_copies:
        copy.start()

    loads[1].wait()
    for copy in map_copies:
        copy.wait_recv()
    place = lax.broadcasted_iota(jnp.int32, (pair, 2 * tok), 0).astype(F32)
    for g in range(2):
        for p in range(8):
            slot = jnp.concatenate([maps[g, 0, p : p + 1, :], maps[g, 1, p : p + 1, :] + cps], axis=1)
            gate = jnp.concatenate([maps[g, 0, 8 + p : 9 + p, :], maps[g, 1, 8 + p : 9 + p, :]], axis=1)
            hit = place == slot
            pick[g, p] = jnp.where(hit, 1.0, 0.0).astype(BF16)
            factor = jnp.sum(jnp.where(hit, gate, 0.0), axis=1, keepdims=True)
            scale[g, p] = jnp.broadcast_to(factor, (pair, 128))

    def lanes(t, size=LANES):
        return pl.ds(pl.multiple_of(t * size, size), size)

    order = (5, 7, 4, 1, 6, 3, 2)
    sent = []

    def dispatch(g, chunk, start, size, whole):
        tokens = slice(None) if whole else block_rows(zl)
        depth = 2 * tok if whole else tok
        weights = pick[g, :, pl.ds(start, size), tokens].reshape(8 * size, depth)
        factor = scale[g, :, pl.ds(start, size), :].reshape(8 * size, 128)[:, :1]

        def tile(t, _):
            out = jnp.dot(weights, og[g, tokens, lanes(t)], preferred_element_type=F32) * factor
            send[g, :, pl.ds(start, size), lanes(t)] = out.astype(BF16).reshape(8, size, LANES)
            return 0

        lax.fori_loop(0, width // LANES, tile, 0)
        copies = []
        for k in order:
            pi, pn = plane_peer(k)
            copy = pltpu.make_async_remote_copy(
                src_ref=send.at[g, pi * 2 + pn, pl.ds(start, size)],
                dst_ref=rows.at[g, mine, pl.ds(start, size)],
                send_sem=ds_sem.at[g, chunk, k], recv_sem=dr_sem.at[g, chunk, k],
                device_id=(pi, m, pn), device_id_type=MESH,
            )
            copy.start()
            copies.append(copy)
        here = pltpu.make_async_copy(
            send.at[g, mine, pl.ds(start, size)], rows.at[g, mine, pl.ds(start, size)], copy_sem.at[g, chunk]
        )
        here.start()
        sent.extend(copies)
        return copies, here

    def forward(g):
        for a in range(4):
            loads[3 + 4 * g + a].wait()

        def tile(t, _):
            out = jnp.dot(
                xs[g].reshape(total, width), wgu[:, lanes(t)], preferred_element_type=F32
            ).reshape(4, 4, cps, LANES)
            for a in range(2):
                for b in range(2):
                    pre[g, :, b * 2 + a, :, lanes(t)] = out[:, a * 2 + b]
            return 0

        lax.fori_loop(0, 2 * hidden_width // LANES, tile, 0)

    def backward(g, arriving):
        for copies, here in arriving:
            for copy in copies:
                copy.wait_recv()
            here.wait()

        def first(t, _):
            size = 256
            at_b = pl.ds(pl.multiple_of(hidden_width + t * size, size), size)
            grad_h = lax.dot_general(
                rows[g].reshape(total, width), wd[lanes(t, size), :], (((1,), (1,)), ((), ())),
                preferred_element_type=F32,
            )
            act_a = pre[g, :, :, :, lanes(t, size)].reshape(total, size)
            act_b = pre[g, :, :, :, at_b].reshape(total, size)
            sigma = jax.nn.sigmoid(act_a)
            silu_a = act_a * sigma
            hid[g, :, lanes(t, size)] = (silu_a * act_b).astype(BF16)
            dgu[:, lanes(t, size)] = (
                grad_h * act_b * sigma * (1.0 + act_a * (1.0 - sigma))
            ).astype(BF16)
            dgu[:, at_b] = (grad_h * silu_a).astype(BF16)
            return 0

        lax.fori_loop(0, hidden_width // 256, first, 0)
        copies = []
        half = width // 2
        for h in range(2):
            def second(t, _):
                out = lax.dot_general(
                    dgu[...], wgu[lanes(t), :], (((1,), (1,)), ((), ())), preferred_element_type=F32
                )
                xs[g, :, :, lanes(t)] = out.astype(BF16).reshape(8, pair, LANES)
                return 0

            lax.fori_loop(h * half // LANES, (h + 1) * half // LANES, second, 0)
            for k in order:
                pi, pn = plane_peer(k)
                copy = pltpu.make_async_remote_copy(
                    src_ref=xs.at[g, pi * 2 + pn, :, pl.ds(h * half, half)],
                    dst_ref=back.at[g, mine, :, pl.ds(h * half, half)],
                    send_sem=cs_sem.at[g, h, k], recv_sem=cr_sem.at[g, h, k],
                    device_id=(pi, m, pn), device_id_type=MESH,
                )
                copy.start()
                copies.append(copy)
        here = pltpu.make_async_copy(xs.at[g, mine], back.at[g, mine], copy_sem.at[g, 2])
        here.start()
        sent.extend(copies)
        return copies, here

    def partial(g, which, put):
        weights = pick[g, :, :, block_rows(which)].reshape(total, tok)

        def tile(t, _):
            put(t, lax.dot_general(
                weights, back[g, :, :, lanes(t)].reshape(total, LANES), (((0,), (0,)), ((), ())),
                preferred_element_type=F32,
            ))
            return 0

        lax.fori_loop(0, width // LANES, tile, 0)

    def keep(t, value):
        own[:, lanes(t)] = value

    def partial_to(j, g, which):
        def put(t, value):
            part[j, :, lanes(t)] = value.astype(BF16)

        partial(g, which, put)
        copy = pltpu.make_async_remote_copy(
            src_ref=part.at[j], dst_ref=got.at[j],
            send_sem=ps_sem.at[j], recv_sem=pr_sem.at[j],
            device_id=(i, z_peer(j), n), device_id_type=MESH,
        )
        copy.start()
        sent.append(copy)
        return copy

    def arrive(copies, here):
        for copy in copies:
            copy.wait_recv()
        here.wait()

    loads[0].wait()
    near = [dispatch(0, 0, early_at, early, False)]
    loads[2].wait()
    forward(0)
    block_copies[0].wait_recv()
    near.append(dispatch(0, 1, late_at, late, True))
    forward(1)
    block_copies[1].wait_recv()
    far = [dispatch(1, 0, early_at, early, False)]
    loads[11].wait()
    near_back = backward(0, near)
    block_copies[2].wait_recv()
    far.append(dispatch(1, 1, late_at, late, True))
    far_back = backward(1, far)
    arrive(*near_back)
    ends = [partial_to(1, 0, 1 - zl)]
    partial(0, zl, keep)

    def gradient(t, _):
        out = lax.dot_general(
            hid[...].reshape(2 * total, hidden_width), rows[:, :, :, lanes(t)].reshape(2 * total, LANES),
            (((0,), (0,)), ((), ())), preferred_element_type=F32,
        )
        down_out[:, lanes(t)] = out.astype(BF16)
        return 0

    lax.fori_loop(0, width // LANES, gradient, 0)
    arrive(*far_back)
    ends.append(partial_to(2, 1, zl))
    ends.append(partial_to(3, 1, 1 - zl))
    for copy in ends:
        copy.wait_recv()
    token_out[...] = (
        own[...] + got[1].astype(F32) + got[2].astype(F32) + got[3].astype(F32)
    ).astype(BF16)
    for copy in map_copies + block_copies + sent:
        copy.wait_send()


def fused(out_grad, maps, inputs, gate_up, down, cps):
    tok, width = out_grad.shape
    hidden_width = down.shape[0]
    pair = 2 * cps
    anywhere = pl.BlockSpec(memory_space=pl.ANY)
    local = pl.BlockSpec(memory_space=pltpu.VMEM)
    dma = pltpu.SemaphoreType.DMA
    return pl.pallas_call(
        functools.partial(fused_kernel, cps),
        out_shape=(
            jax.ShapeDtypeStruct((tok, width), BF16),
            jax.ShapeDtypeStruct((hidden_width, width), BF16),
        ),
        in_specs=[anywhere] * 5,
        out_specs=(local, local),
        scratch_shapes=[
            pltpu.VMEM((2, 2 * tok, width), BF16),
            pltpu.VMEM((2, 2, 16, tok), F32),
            pltpu.VMEM((2, 8, pair, 2 * tok), BF16),
            pltpu.VMEM((2, 8, pair, 128), F32),
            pltpu.VMEM((2, 8, pair, width), BF16),
            pltpu.VMEM((2, 8, pair, width), BF16),
            pltpu.VMEM((2, 8, pair, width), BF16),
            pltpu.VMEM((2, 8, pair, width), BF16),
            pltpu.VMEM((2, 4, 4, cps, 2 * hidden_width), F32),
            pltpu.VMEM((width, 2 * hidden_width), BF16),
            pltpu.VMEM((hidden_width, width), BF16),
            pltpu.VMEM((8 * pair, 2 * hidden_width), BF16),
            pltpu.VMEM((2, 8 * pair, hidden_width), BF16),
            pltpu.VMEM((tok, width), F32),
            pltpu.VMEM((4, tok, width), BF16),
            pltpu.VMEM((4, tok, width), BF16),
            dma((12,)), dma((2, 3)), dma((4,)), dma((4,)), dma((4,)), dma((4,)),
            dma((2, 2, 8)), dma((2, 2, 8)), dma((2, 2, 8)), dma((2, 2, 8)), dma((4,)), dma((4,)),
        ],
        compiler_params=pltpu.CompilerParams(
            collective_id=0, has_side_effects=True, vmem_limit_bytes=62 * 1024 * 1024
        ),
    )(out_grad, maps, inputs, gate_up, down)


def routing_maps(ids, gates, count):
    tok = ids.shape[0]
    chosen = ids[:, :, None] == jnp.arange(count, dtype=jnp.int32)
    named = jnp.any(chosen, axis=1)
    before = jnp.arange(tok)[:, None] > jnp.arange(tok)[None, :]
    slot = jnp.dot(
        before.astype(jnp.bfloat16), named.astype(jnp.bfloat16), preferred_element_type=jnp.float32
    )
    slot = jnp.where(named, slot, -1024.0)
    gate = jnp.sum(jnp.where(chosen, gates[:, :, None], 0.0), axis=1)
    return slot.T, gate.T


def per_device(out_grad, expert_ids, gates, expert_input, gate_up_weight, down_weight):
    inner, major, minor = lax.axis_size("i"), lax.axis_size("m"), lax.axis_size("n")
    plane = inner * minor
    tok = expert_ids.shape[0]
    sources, _, cps, width = expert_input.shape
    slot, gate = routing_maps(expert_ids, gates, sources)
    if (inner, major, minor, tok, cps % 8) == (4, 4, 2, 128, 0):
        maps = jnp.stack([slot, gate]).reshape(2, inner, major, minor, tok).transpose(2, 0, 1, 3, 4)
        token_grad, down_grad = fused(
            out_grad, maps.reshape(major, 2 * plane, tok),
            expert_input.reshape(inner, major, minor * cps, width), gate_up_weight[0], down_weight[0], cps,
        )
        return token_grad, down_grad[None]
    maps = jnp.stack([slot, gate]).reshape(2, inner, major, minor, tok).transpose(2, 0, 1, 3, 4)
    maps = lax.all_to_all(maps, "m", split_axis=0, concat_axis=0, tiled=True)
    slot, gate = maps[:, 0].reshape(major, plane, tok), maps[:, 1].reshape(major, plane, tok)
    blocks = lax.all_gather(out_grad, "m")
    pick = slot[:, :, None, :] == jnp.arange(cps, dtype=jnp.float32)[:, None]
    scale = jnp.sum(jnp.where(pick, gate[:, :, None, :], 0.0), axis=-1)
    pick = pick.astype(jnp.bfloat16)
    rows = jnp.einsum("mpct,mtd->pmcd", pick, blocks, preferred_element_type=jnp.float32)
    rows = (rows * scale.transpose(1, 0, 2)[..., None]).astype(jnp.bfloat16)
    rows = lax.all_to_all(rows, PLANE, split_axis=0, concat_axis=0, tiled=True)
    rows = rows.reshape(sources * cps, width)
    inputs = expert_input.reshape(inner, major, minor, cps, width).transpose(0, 2, 1, 3, 4)
    inputs = inputs.reshape(sources * cps, width)

    gate_up, down = gate_up_weight[0], down_weight[0]
    hidden_width = down.shape[0]
    pre = jnp.dot(inputs, gate_up, preferred_element_type=jnp.float32)
    act_a, act_b = pre[:, :hidden_width], pre[:, hidden_width:]
    sigma = jax.nn.sigmoid(act_a)
    silu_a = act_a * sigma
    hidden = (silu_a * act_b).astype(jnp.bfloat16)
    grad_h = lax.dot_general(
        rows, down, (((1,), (1,)), ((), ())), preferred_element_type=jnp.float32
    )
    grad_a = grad_h * act_b * sigma * (1.0 + act_a * (1.0 - sigma))
    grad_gu = jnp.concatenate([grad_a, grad_h * silu_a], axis=1).astype(jnp.bfloat16)
    slot_grad = lax.dot_general(
        grad_gu, gate_up, (((1,), (1,)), ((), ())), preferred_element_type=jnp.float32
    ).astype(jnp.bfloat16)
    down_grad = lax.dot_general(
        hidden, rows, (((0,), (0,)), ((), ())), preferred_element_type=jnp.float32
    ).astype(jnp.bfloat16)

    back = slot_grad.reshape(plane, major, cps, width)
    back = lax.all_to_all(back, PLANE, split_axis=0, concat_axis=0, tiled=True)
    part = jnp.einsum("mpct,pmcd->mtd", pick, back, preferred_element_type=jnp.float32)
    part = part.astype(jnp.bfloat16)
    part = lax.all_to_all(part, "m", split_axis=0, concat_axis=0, tiled=True)
    token_grad = jnp.sum(part.astype(jnp.float32), axis=0).astype(jnp.bfloat16)
    return token_grad, down_grad[None]


def solution(mesh):
    inner, outer = mesh.devices.shape
    major = 4
    fine = Mesh(mesh.devices.reshape(inner, major, outer // major), ("i", "m", "n"))
    every = ("i", "m", "n")
    placed = (
        P(every, None),
        P(every, None),
        P(every, None),
        P(None, every, None, None),
        P(every, None, None),
        P(every, None, None),
    )
    return jax.shard_map(
        per_device,
        mesh=fine,
        in_specs=placed,
        out_specs=(P(every, None), P(every, None, None)),
        check_vma=False,
    )
```

profile of v0, /device:TPU:8, one launch (start us, length us, event | category | flops | bytes accessed | tf_op | source)
XLA Modules:
  0.0 189.2 jit_solution(15410615966819649432)
XLA Ops:
  0.6 0.7 fusion
  1.3 0.1 convolution_select_fusion
  1.5 0.7 select_reduce_fusion
  2.2 0.6 copy.14
  2.9 180.5 %shard_map.77 = (bf16[128,2048]{1,0:T(8,128)(2,1)}, bf16[768,2048]{1,0:T(8,128)(2,1)}) custom-call(bf16[128,2048]{1,0:T(8,128)(2,1)} %og_in.1, f32[4,16,128]{2,1,0:T(8,128)} %bitcast.18, bf16[4,4,80,2048]{3,2,1,0:T(8,128)(2,1)} %bitcast.15, bf16[2048,1536]{1,0:T(8,128)(2,1)} %bitcast.14, bf16[768,2048]{1,0:T(8,128)(2,1)} %bitcast.17), custom_call_target="tpu_custom_call" | custom-call | tf_op jit(solution)/shard_map/pallas_call | solution.py:285
  183.4 1.9 copy.17
  185.2 4.0 %copy.18 = bf16[1,768,2048]{2,1,0:T(8,128)(2,1)} copy(bf16[1,768,2048]{2,1,0:T(8,128)(2,1)} %bitcast.16) | data formatting | bytes 6291456
  (1 shorter events, 0.0 us)
where the time goes:
time: 189 us
  Pallas kernels  180 us (95%)
  local copies, waits for them, and re-layouts  6.48 us (3%)
    pallas_call x1, Pallas kernels, fused(): pl.pallas_call(functools.partial(fused_kernel, cps), out_shape=(jax.Shape...  180 us
    unnamed x2, local copies, waits for them, and re-layouts  5.85 us

commit v1 on v0

--- a/solution.py
+++ b/solution.py
@@ -15,7 +15,7 @@
 
 def fused_kernel(
     cps, og_in, maps_in, x_in, wgu_in, wd_in, token_out, down_out,
-    og, maps, pick, scale, send, rows, xs, back, pre, wgu, wd, dgu, hid, own, part, got,
+    og, maps, pick, scale, send, rows, xs, back, pre, wgu, wd, dgu, hid, own, hold, part, got,
     load_sem, copy_sem, zs_sem, zr_sem, ms_sem, mr_sem, ds_sem, dr_sem, cs_sem, cr_sem, ps_sem, pr_sem,
 ):
     i, m, n = lax.axis_index("i"), lax.axis_index("m"), lax.axis_index("n")
@@ -79,13 +79,19 @@
         )
         block_copies.append(
             pltpu.make_async_remote_copy(
-                src_ref=og_in, dst_ref=og.at[j // 2, block_rows(zl)],
+                src_ref=og.at[1, block_rows(zl)] if j == 3 else og_in, dst_ref=og.at[j // 2, block_rows(zl)],
                 send_sem=zs_sem.at[j], recv_sem=zr_sem.at[j],
-                device_id=(i, there, n), device_id_type=MESH,
-            )
-        )
-    for copy in map_copies + block_copies:
+                device_id=(i, z_peer(j % 2 or 2), n), device_id_type=MESH,
+            )
+        )
+    near_copy, cross_copy, forward_copy = block_copies
+    for copy in map_copies:
         copy.start()
+    near_copy.start()
+
+    @pl.when(zh + zl == 1)
+    def _():
+        cross_copy.start()
 
     loads[1].wait()
     for copy in map_copies:
@@ -105,6 +111,7 @@
 
     order = (5, 7, 4, 1, 6, 3, 2)
     sent = []
+    half = width // 2
 
     def dispatch(g, chunk, start, size, whole):
         tokens = slice(None) if whole else block_rows(zl)
@@ -151,7 +158,7 @@
 
         lax.fori_loop(0, 2 * hidden_width // LANES, tile, 0)
 
-    def backward(g, arriving):
+    def backward(g, arriving, go):
         for copies, here in arriving:
             for copy in copies:
                 copy.wait_recv()
@@ -177,7 +184,6 @@
 
         lax.fori_loop(0, hidden_width // 256, first, 0)
         copies = []
-        half = width // 2
         for h in range(2):
             def second(t, _):
                 out = lax.dot_general(
@@ -187,22 +193,28 @@
                 return 0
 
             lax.fori_loop(h * half // LANES, (h + 1) * half // LANES, second, 0)
-            for k in order:
-                pi, pn = plane_peer(k)
-                copy = pltpu.make_async_remote_copy(
-                    src_ref=xs.at[g, pi * 2 + pn, :, pl.ds(h * half, half)],
-                    dst_ref=back.at[g, mine, :, pl.ds(h * half, half)],
-                    send_sem=cs_sem.at[g, h, k], recv_sem=cr_sem.at[g, h, k],
-                    device_id=(pi, m, pn), device_id_type=MESH,
-                )
-                copy.start()
-                copies.append(copy)
-        here = pltpu.make_async_copy(xs.at[g, mine], back.at[g, mine], copy_sem.at[g, 2])
+            if go:
+                copies.append(hand_back(g, h))
+        return copies
+
+    def hand_back(g, h):
+        cols = pl.ds(h * half, half)
+        copies = []
+        for k in order:
+            pi, pn = plane_peer(k)
+            copy = pltpu.make_async_remote_copy(
+                src_ref=xs.at[g, pi * 2 + pn, :, cols], dst_ref=back.at[g, mine, :, cols],
+                send_sem=cs_sem.at[g, h, k], recv_sem=cr_sem.at[g, h, k],
+                device_id=(pi, m, pn), device_id_type=MESH,
+            )
+            copy.start()
+            copies.append(copy)
+        here = pltpu.make_async_copy(xs.at[g, mine, :, cols], back.at[g, mine, :, cols], copy_sem.at[g, 2 + h])
         here.start()
         sent.extend(copies)
         return copies, here
 
-    def partial(g, which, put):
+    def partial(g, which, h, put):
         weights = pick[g, :, :, block_rows(which)].reshape(total, tok)
 
         def tile(t, _):
@@ -212,24 +224,49 @@
             ))
             return 0
 
-        lax.fori_loop(0, width // LANES, tile, 0)
+        lax.fori_loop(h * half // LANES, (h + 1) * half // LANES, tile, 0)
 
     def keep(t, value):
         own[:, lanes(t)] = value
 
-    def partial_to(j, g, which):
-        def put(t, value):
-            part[j, :, lanes(t)] = value.astype(BF16)
-
-        partial(g, which, put)
+    def set_aside(t, value):
+        hold[:, lanes(t)] = value
+
+    def ship(j, h, to):
+        cols = pl.ds(h * half, half)
         copy = pltpu.make_async_remote_copy(
-            src_ref=part.at[j], dst_ref=got.at[j],
-            send_sem=ps_sem.at[j], recv_sem=pr_sem.at[j],
-            device_id=(i, z_peer(j), n), device_id_type=MESH,
+            src_ref=part.at[j, :, cols], dst_ref=got.at[j, :, cols],
+            send_sem=ps_sem.at[j, h], recv_sem=pr_sem.at[j, h],
+            device_id=(i, z_peer(to), n), device_id_type=MESH,
         )
         copy.start()
         sent.append(copy)
         return copy
+
+    def near_part(h, arriving):
+        arrive(*arriving)
+
+        def put(t, value):
+            part[1, :, lanes(t)] = value.astype(BF16)
+
+        partial(0, 1 - zl, h, put)
+        copy = ship(1, h, 1)
+        partial(0, zl, h, keep)
+        return copy
+
+    def far_part(h, arriving):
+        arrive(*arriving)
+
+        def put(t, value):
+            part[3, :, lanes(t)] = value.astype(BF16)
+
+        partial(1, 1 - zl, h, put)
+        copy = ship(3, h, 1)
+        partial(1, zl, h, set_aside)
+        copy.wait_recv()
+        cols = pl.ds(h * half, half)
+        part[2, :, cols] = (hold[:, cols] + got[3, :, cols].astype(F32)).astype(BF16)
+        return ship(2, h, 2)
 
     def arrive(copies, here):
         for copy in copies:
@@ -240,19 +277,26 @@
     near = [dispatch(0, 0, early_at, early, False)]
     loads[2].wait()
     forward(0)
-    block_copies[0].wait_recv()
+    near_copy.wait_send()
+
+    @pl.when(zh + zl != 1)
+    def _():
+        cross_copy.start()
+
+    near_copy.wait_recv()
     near.append(dispatch(0, 1, late_at, late, True))
     forward(1)
-    block_copies[1].wait_recv()
+    cross_copy.wait_recv()
+    forward_copy.start()
     far = [dispatch(1, 0, early_at, early, False)]
     loads[11].wait()
-    near_back = backward(0, near)
-    block_copies[2].wait_recv()
+    backward(0, near, False)
+    forward_copy.wait_recv()
     far.append(dispatch(1, 1, late_at, late, True))
-    far_back = backward(1, far)
-    arrive(*near_back)
-    ends = [partial_to(1, 0, 1 - zl)]
-    partial(0, zl, keep)
+    near_back = [hand_back(0, 0)]
+    far_back = backward(1, far, True)
+    near_back.append(hand_back(0, 1))
+    ends = [near_part(0, near_back[0])]
 
     def gradient(t, _):
         out = lax.dot_general(
@@ -263,15 +307,15 @@
         return 0
 
     lax.fori_loop(0, width // LANES, gradient, 0)
-    arrive(*far_back)
-    ends.append(partial_to(2, 1, zl))
-    ends.append(partial_to(3, 1, 1 - zl))
+    ends.append(far_part(0, far_back[0]))
+    ends.append(far_part(1, far_back[1]))
+    ends.append(near_part(1, near_back[1]))
     for copy in ends:
         copy.wait_recv()
     token_out[...] = (
-        own[...] + got[1].astype(F32) + got[2].astype(F32) + got[3].astype(F32)
+        own[...] + got[1].astype(F32) + got[2].astype(F32)
     ).astype(BF16)
-    for copy in map_copies + block_copies + sent:
+    for copy in map_copies + [cross_copy, forward_copy] + sent:
         copy.wait_send()
 
 
@@ -305,10 +349,11 @@
             pltpu.VMEM((8 * pair, 2 * hidden_width), BF16),
             pltpu.VMEM((2, 8 * pair, hidden_width), BF16),
             pltpu.VMEM((tok, width), F32),
+            pltpu.VMEM((tok, width), F32),
             pltpu.VMEM((4, tok, width), BF16),
             pltpu.VMEM((4, tok, width), BF16),
-            dma((12,)), dma((2, 3)), dma((4,)), dma((4,)), dma((4,)), dma((4,)),
-            dma((2, 2, 8)), dma((2, 2, 8)), dma((2, 2, 8)), dma((2, 2, 8)), dma((4,)), dma((4,)),
+            dma((12,)), dma((2, 4)), dma((4,)), dma((4,)), dma((4,)), dma((4,)),
+            dma((2, 2, 8)), dma((2, 2, 8)), dma((2, 2, 8)), dma((2, 2, 8)), dma((4, 2)), dma((4, 2)),
         ],
         compiler_params=pltpu.CompilerParams(
             collective_id=0, has_side_effects=True, vmem_limit_bytes=62 * 1024 * 1024

time: 189 us -> 162 us (0.86)
  the two profiles are of different devices: /device:TPU:8 before, /device:TPU:0 now
where the time goes in v1:
time: 162 us; the launch traced here: 161 us
  Pallas kernels  153 us (94%)
  local copies, waits for them, and re-layouts  6.48 us (4%)
    pallas_call x1, Pallas kernels, fused(): pl.pallas_call(functools.partial(fused_kernel, cps), out_shape=(jax.Shape...  153 us
    unnamed x2, local copies, waits for them, and re-layouts  5.85 us

profile of v1, /device:TPU:0, one launch (start us, length us, event | category | flops | bytes accessed | tf_op | source)
XLA Modules:
  0.0 161.2 jit_solution(11410199112869400064)
XLA Ops:
  0.6 0.7 fusion
  1.3 0.1 convolution_select_fusion
  1.5 0.7 select_reduce_fusion
  2.2 0.6 copy.14
  2.9 152.5 %shard_map.77 = (bf16[128,2048]{1,0:T(8,128)(2,1)}, bf16[768,2048]{1,0:T(8,128)(2,1)}) custom-call(bf16[128,2048]{1,0:T(8,128)(2,1)} %og_in.1, f32[4,16,128]{2,1,0:T(8,128)} %bitcast.18, bf16[4,4,80,2048]{3,2,1,0:T(8,128)(2,1)} %bitcast.15, bf16[2048,1536]{1,0:T(8,128)(2,1)} %bitcast.14, bf16[768,2048]{1,0:T(8,128)(2,1)} %bitcast.17), custom_call_target="tpu_custom_call" | custom-call | tf_op jit(solution)/shard_map/pallas_call | solution.py:329
  155.4 1.9 %copy.17 = bf16[128,2048]{1,0:T(8,128)(2,1)} copy(bf16[128,2048]{1,0:T(8,128)(2,1)} %get-tuple-element.8) | data formatting | bytes 1048576
  157.3 4.0 %copy.18 = bf16[1,768,2048]{2,1,0:T(8,128)(2,1)} copy(bf16[1,768,2048]{2,1,0:T(8,128)(2,1)} %bitcast.16) | data formatting | bytes 6291456
  (1 shorter events, 0.0 us)

commit v2 on v1

--- a/solution.py
+++ b/solution.py
@@ -15,7 +15,7 @@
 
 def fused_kernel(
     cps, og_in, maps_in, x_in, wgu_in, wd_in, token_out, down_out,
-    og, maps, pick, scale, send, rows, xs, back, pre, wgu, wd, dgu, hid, own, hold, part, got,
+    og, maps, pick, scale, send, rows, xs, back, pre, wgu, wd, dgu, hid, down, own, hold, part, got,
     load_sem, copy_sem, zs_sem, zr_sem, ms_sem, mr_sem, ds_sem, dr_sem, cs_sem, cr_sem, ps_sem, pr_sem,
 ):
     i, m, n = lax.axis_index("i"), lax.axis_index("m"), lax.axis_index("n")
@@ -65,6 +65,19 @@
     for k in range(1, 8):
         pi, pn = plane_peer(k)
         pl.semaphore_signal(barrier, inc=1, device_id=(pi, m, pn), device_id_type=MESH)
+
+    place = lax.broadcasted_iota(jnp.int32, (pair, tok), 0).astype(F32)
+
+    def choose(g, which, first):
+        for p in range(8):
+            hit = place == maps[g, which, p : p + 1, :] + (cps * which).astype(F32)
+            pick[g, p, :, block_rows(which)] = jnp.where(hit, 1.0, 0.0).astype(BF16)
+            factor = jnp.sum(jnp.where(hit, maps[g, which, 8 + p : 9 + p, :], 0.0), axis=1, keepdims=True)
+            factor = jnp.broadcast_to(factor, (pair, 128))
+            scale[g, p] = factor if first else scale[g, p] + factor
+
+    loads[1].wait()
+    choose(0, zl, True)
     pl.semaphore_wait(barrier, 10)
 
     map_copies, block_copies = [], []
@@ -92,19 +105,6 @@
     @pl.when(zh + zl == 1)
     def _():
         cross_copy.start()
-
-    loads[1].wait()
-    for copy in map_copies:
-        copy.wait_recv()
-    place = lax.broadcasted_iota(jnp.int32, (pair, 2 * tok), 0).astype(F32)
-    for g in range(2):
-        for p in range(8):
-            slot = jnp.concatenate([maps[g, 0, p : p + 1, :], maps[g, 1, p : p + 1, :] + cps], axis=1)
-            gate = jnp.concatenate([maps[g, 0, 8 + p : 9 + p, :], maps[g, 1, 8 + p : 9 + p, :]], axis=1)
-            hit = place == slot
-            pick[g, p] = jnp.where(hit, 1.0, 0.0).astype(BF16)
-            factor = jnp.sum(jnp.where(hit, gate, 0.0), axis=1, keepdims=True)
-            scale[g, p] = jnp.broadcast_to(factor, (pair, 128))
 
     def lanes(t, size=LANES):
         return pl.ds(pl.multiple_of(t * size, size), size)
@@ -275,6 +275,11 @@
 
     loads[0].wait()
     near = [dispatch(0, 0, early_at, early, False)]
+    for copy in map_copies:
+        copy.wait_recv()
+    choose(0, 1 - zl, False)
+    choose(1, zl, True)
+    choose(1, 1 - zl, False)
     loads[2].wait()
     forward(0)
     near_copy.wait_send()
@@ -290,23 +295,24 @@
     forward_copy.start()
     far = [dispatch(1, 0, early_at, early, False)]
     loads[11].wait()
-    backward(0, near, False)
     forward_copy.wait_recv()
     far.append(dispatch(1, 1, late_at, late, True))
+    backward(0, near, False)
     near_back = [hand_back(0, 0)]
     far_back = backward(1, far, True)
     near_back.append(hand_back(0, 1))
-    ends = [near_part(0, near_back[0])]
-
     def gradient(t, _):
         out = lax.dot_general(
             hid[...].reshape(2 * total, hidden_width), rows[:, :, :, lanes(t)].reshape(2 * total, LANES),
             (((0,), (0,)), ((), ())), preferred_element_type=F32,
         )
-        down_out[:, lanes(t)] = out.astype(BF16)
+        down[:, lanes(t)] = out.astype(BF16)
         return 0
 
     lax.fori_loop(0, width // LANES, gradient, 0)
+    result = pltpu.make_async_copy(down, down_out, load_sem.at[12])
+    result.start()
+    ends = [near_part(0, near_back[0])]
     ends.append(far_part(0, far_back[0]))
     ends.append(far_part(1, far_back[1]))
     ends.append(near_part(1, near_back[1]))
@@ -315,6 +321,7 @@
     token_out[...] = (
         own[...] + got[1].astype(F32) + got[2].astype(F32)
     ).astype(BF16)
+    result.wait()
     for copy in map_copies + [cross_copy, forward_copy] + sent:
         copy.wait_send()
 
@@ -333,7 +340,7 @@
             jax.ShapeDtypeStruct((hidden_width, width), BF16),
         ),
         in_specs=[anywhere] * 5,
-        out_specs=(local, local),
+        out_specs=(local, anywhere),
         scratch_shapes=[
             pltpu.VMEM((2, 2 * tok, width), BF16),
             pltpu.VMEM((2, 2, 16, tok), F32),
@@ -348,11 +355,12 @@
             pltpu.VMEM((hidden_width, width), BF16),
             pltpu.VMEM((8 * pair, 2 * hidden_width), BF16),
             pltpu.VMEM((2, 8 * pair, hidden_width), BF16),
+            pltpu.VMEM((hidden_width, width), BF16),
             pltpu.VMEM((tok, width), F32),
             pltpu.VMEM((tok, width), F32),
             pltpu.VMEM((4, tok, width), BF16),
             pltpu.VMEM((4, tok, width), BF16),
-            dma((12,)), dma((2, 4)), dma((4,)), dma((4,)), dma((4,)), dma((4,)),
+            dma((13,)), dma((2, 4)), dma((4,)), dma((4,)), dma((4,)), dma((4,)),
             dma((2, 2, 8)), dma((2, 2, 8)), dma((2, 2, 8)), dma((2, 2, 8)), dma((4, 2)), dma((4, 2)),
         ],
         compiler_params=pltpu.CompilerParams(

time: 162 us -> 161 us (level)
  the two profiles are of different devices: /device:TPU:0 before, /device:TPU:10 now
where the time goes in v2:
time: 161 us
  Pallas kernels  152 us (94%)
  local copies, waits for them, and re-layouts  6.48 us (4%)
    pallas_call x1, Pallas kernels, fused(): pl.pallas_call(functools.partial(fused_kernel, cps), out_shape=(jax.Shape...  152 us
    unnamed x2, local copies, waits for them, and re-layouts  5.85 us

profile of v2, /device:TPU:10, one launch (start us, length us, event | category | flops | bytes accessed | tf_op | source)
XLA Modules:
  0.0 160.6 jit_solution(6286039040081077109)
XLA Ops:
  0.6 0.7 fusion
  1.3 0.1 convolution_select_fusion
  1.5 0.7 select_reduce_fusion
  2.2 0.6 copy.14
  2.9 151.9 %shard_map.77 = (bf16[128,2048]{1,0:T(8,128)(2,1)}, bf16[768,2048]{1,0:T(8,128)(2,1)}) custom-call(bf16[128,2048]{1,0:T(8,128)(2,1)} %og_in.1, f32[4,16,128]{2,1,0:T(8,128)} %bitcast.18, bf16[4,4,80,2048]{3,2,1,0:T(8,128)(2,1)} %bitcast.15, bf16[2048,1536]{1,0:T(8,128)(2,1)} %bitcast.14, bf16[768,2048]{1,0:T(8,128)(2,1)} %bitcast.17), custom_call_target="tpu_custom_call" | custom-call | tf_op jit(solution)/shard_map/pallas_call | solution.py:336
  154.8 1.9 %copy.17 = bf16[128,2048]{1,0:T(8,128)(2,1)} copy(bf16[128,2048]{1,0:T(8,128)(2,1)} %get-tuple-element.8) | data formatting | bytes 1048576
  156.6 4.0 %copy.18 = bf16[1,768,2048]{2,1,0:T(8,128)(2,1)} copy(bf16[1,768,2048]{2,1,0:T(8,128)(2,1)} %bitcast.16) | data formatting | bytes 6291456
  (1 shorter events, 0.0 us)

commit v3 on v2

--- a/solution.py
+++ b/solution.py
@@ -163,6 +163,8 @@
             for copy in copies:
                 copy.wait_recv()
             here.wait()
+        if go:
+            near_back.append(hand_back(0, 0))
 
         def first(t, _):
             size = 256
@@ -254,9 +256,7 @@
         partial(0, zl, h, keep)
         return copy
 
-    def far_part(h, arriving):
-        arrive(*arriving)
-
+    def far_part(h):
         def put(t, value):
             part[3, :, lanes(t)] = value.astype(BF16)
 
@@ -280,8 +280,6 @@
     choose(0, 1 - zl, False)
     choose(1, zl, True)
     choose(1, 1 - zl, False)
-    loads[2].wait()
-    forward(0)
     near_copy.wait_send()
 
     @pl.when(zh + zl != 1)
@@ -290,17 +288,18 @@
 
     near_copy.wait_recv()
     near.append(dispatch(0, 1, late_at, late, True))
-    forward(1)
+    loads[2].wait()
+    forward(0)
     cross_copy.wait_recv()
     forward_copy.start()
     far = [dispatch(1, 0, early_at, early, False)]
+    forward(1)
     loads[11].wait()
     forward_copy.wait_recv()
     far.append(dispatch(1, 1, late_at, late, True))
     backward(0, near, False)
-    near_back = [hand_back(0, 0)]
+    near_back = []
     far_back = backward(1, far, True)
-    near_back.append(hand_back(0, 1))
     def gradient(t, _):
         out = lax.dot_general(
             hid[...].reshape(2 * total, hidden_width), rows[:, :, :, lanes(t)].reshape(2 * total, LANES),
@@ -313,8 +312,11 @@
     result = pltpu.make_async_copy(down, down_out, load_sem.at[12])
     result.start()
     ends = [near_part(0, near_back[0])]
-    ends.append(far_part(0, far_back[0]))
-    ends.append(far_part(1, far_back[1]))
+    arrive(*far_back[0])
+    near_back.append(hand_back(0, 1))
+    ends.append(far_part(0))
+    arrive(*far_back[1])
+    ends.append(far_part(1))
     ends.append(near_part(1, near_back[1]))
     for copy in ends:
         copy.wait_recv()

time: 161 us -> 163 us (1.012)
  the two profiles are of different devices: /device:TPU:10 before, /device:TPU:0 now
where the time goes in v3:
time: 163 us
  Pallas kernels  154 us (94%)
  local copies, waits for them, and re-layouts  6.48 us (4%)
    pallas_call x1, Pallas kernels, fused(): pl.pallas_call(functools.partial(fused_kernel, cps), out_shape=(jax.Shape...  154 us
    unnamed x2, local copies, waits for them, and re-layouts  5.85 us

profile of v3, /device:TPU:0, one launch (start us, length us, event | category | flops | bytes accessed | tf_op | source)
XLA Modules:
  0.0 163.1 jit_solution(13712673862586169066)
XLA Ops:
  0.6 0.7 fusion
  1.3 0.1 convolution_select_fusion
  1.5 0.7 select_reduce_fusion
  2.2 0.6 copy.14
  2.9 154.3 %shard_map.77 = (bf16[128,2048]{1,0:T(8,128)(2,1)}, bf16[768,2048]{1,0:T(8,128)(2,1)}) custom-call(bf16[128,2048]{1,0:T(8,128)(2,1)} %og_in.1, f32[4,16,128]{2,1,0:T(8,128)} %bitcast.18, bf16[4,4,80,2048]{3,2,1,0:T(8,128)(2,1)} %bitcast.15, bf16[2048,1536]{1,0:T(8,128)(2,1)} %bitcast.14, bf16[768,2048]{1,0:T(8,128)(2,1)} %bitcast.17), custom_call_target="tpu_custom_call" | custom-call | tf_op jit(solution)/shard_map/pallas_call | solution.py:338
  157.2 1.9 %copy.17 = bf16[128,2048]{1,0:T(8,128)(2,1)} copy(bf16[128,2048]{1,0:T(8,128)(2,1)} %get-tuple-element.8) | data formatting | bytes 1048576
  159.1 4.0 %copy.18 = bf16[1,768,2048]{2,1,0:T(8,128)(2,1)} copy(bf16[1,768,2048]{2,1,0:T(8,128)(2,1)} %bitcast.16) | data formatting | bytes 6291456
  (1 shorter events, 0.0 us)
